TPU v7x, 32 devices: a whole 2x2x4 slice. The times are simulated.
32 devices in a mesh: groups: 2 (over y), dp: 8 (over z, x), tensor: 2 (over core).
Axes of the slice: x: 2, y: 2, z: 4, core: 2. Of those that a mesh axis runs over, the one named last changes fastest.
Arguments:
- tokens: bfloat16 [6144, 5120], P(('groups', 'dp'), 'tensor'), parts along dimension 0, may hold values from -6 to 6
- expert_ids: int32 [6144, 6], P(('groups', 'dp')), parts along dimension 0, may hold values from 0 to 159, as said below
- combine: float32 [6144, 6], P(('groups', 'dp')), parts along dimension 0, may hold values from 0.1 to 1
- row_list: int32 [6144], P(('groups', 'dp')), parts along dimension 0, may hold values from -1 to 383, as said below
- gate_q: bfloat16 [5120, 768], P('dp', 'tensor'), may hold values from -0.078125 to 0.078125
- gate_scale: float32 [5120, 6], P('dp', 'tensor'), may hold values from 0.3 to 3
- up_q: bfloat16 [5120, 768], P('dp', 'tensor'), may hold values from -0.078125 to 0.078125
- up_scale: float32 [5120, 6], P('dp', 'tensor'), may hold values from 0.3 to 3
- down_q: bfloat16 [768, 5120], P('tensor', 'dp'), may hold values from -0.21875 to 0.21875
- down_scale: float32 [6, 5120], P('tensor', 'dp'), may hold values from 0.3 to 3
Outputs:
- expert_output: bfloat16 [6144, 5120], P(('groups', 'dp'), 'tensor'), parts along dimension 0
There are 2 independent parts, one for each index of `groups`. A program takes and returns all parts, laid end to end along the dimension named above; an argument that names none is the same for every part. Nothing has to cross between parts.
Inputs may be any that keep to these rules, and one draw needn't show every extreme that they name: `expert_ids`: each row holds 6 different expert numbers; expert 0 is the expert whose weights are given. `row_list`: each index of dp has 384 entries: in ascending order the local rows (0 to 383 in that index's block of tokens) whose expert_ids name expert 0, then -1. The last index of dp lists all 384 of its rows.
All inputs are finite; a program needn't handle non-finite values.
Results may differ from a plain program's by a relative error of at most 0.02.
Values may be sent and summed in bfloat16 or wider, within the bound.
A program may use at most 128 MiB of HBM per device.

v0:
```python
import jax
import jax.numpy as jnp
from jax import lax
from jax.sharding import PartitionSpec as P


def dequantize(values, scales, tile_axis):
    tile_len = values.shape[tile_axis] // scales.shape[tile_axis]
    return (values.astype(jnp.float32) * jnp.repeat(scales, tile_len, axis=tile_axis)).astype(
        jnp.bfloat16
    )


def body(
    tokens, expert_ids, combine, row_list, gate_q, gate_scale, up_q, up_scale, down_q, down_scale
):
    full_tokens = lax.all_gather(tokens, "tensor", axis=1, tiled=True)
    listed = row_list >= 0
    safe_rows = jnp.maximum(row_list, 0)
    routed_rows = jnp.take(full_tokens, safe_rows, axis=0)
    picked_ids = jnp.take(expert_ids, safe_rows, axis=0)
    picked_weights = jnp.take(combine, safe_rows, axis=0)
    slot_hits = jnp.where(picked_ids == 0, picked_weights, jnp.zeros_like(picked_weights))
    row_weight = jnp.where(listed, jnp.sum(slot_hits, axis=1), jnp.zeros_like(slot_hits[:, 0]))

    def add_ready(weights):
        return jnp.dot(routed_rows, weights, preferred_element_type=jnp.float32)

    gate_local = dequantize(gate_q, gate_scale, 1)
    up_local = dequantize(up_q, up_scale, 1)
    gate_act = add_ready(lax.all_gather(gate_local, "dp", axis=0, tiled=True))
    up_act = add_ready(lax.all_gather(up_local, "dp", axis=0, tiled=True))
    hidden = (jax.nn.silu(gate_act) * up_act).astype(jnp.bfloat16)
    down_w = lax.all_gather(dequantize(down_q, down_scale, 0), "dp", axis=1, tiled=True)
    partial_value = (
        jnp.dot(hidden, down_w, preferred_element_type=jnp.float32) * row_weight[:, None]
    )
    shares = lax.psum_scatter(
        partial_value.astype(jnp.bfloat16), "tensor", scatter_dimension=1, tiled=True
    ).astype(jnp.float32)
    target_row = jnp.where(listed, row_list, row_list.shape[0])
    return (
        jnp.zeros(shares.shape, jnp.bfloat16)
        .at[target_row]
        .set(shares.astype(jnp.bfloat16), mode="drop")
    )


def solution(mesh):
    placed = (
        P(("groups", "dp"), "tensor"),
        P(("groups", "dp"), None),
        P(("groups", "dp"), None),
        P(("groups", "dp")),
        P("dp", "tensor"),
        P("dp", "tensor"),
        P("dp", "tensor"),
        P("dp", "tensor"),
        P("tensor", "dp"),
        P("tensor", "dp"),
    )
    return jax.shard_map(
        body, mesh=mesh, in_specs=placed, out_specs=P(("groups", "dp"), "tensor"), check_vma=False
    )
```

profile of v0, /device:TPU:1, one launch (start us, length us, event | category | flops | bytes accessed | tf_op | source)
XLA Modules:
  0.0 273.4 jit_solution(4568963529668904327)
XLA Ops:
  6.5 0.0 copy-start
  6.5 0.0 copy-start.5
  6.5 0.0 copy-start.6
  6.5 0.0 copy-start.1
  6.5 0.0 copy-start.3
  6.5 0.0 copy-start.4
  6.6 0.0 copy-start.2
  6.6 0.0 all-gather.5.cloned.1.call-start
  6.6 0.7 all-gather.5.cloned.1.call-update
  7.3 0.0 all-gather.7.cloned.1.call-start
  7.3 1.3 copy.15
  8.6 1.6 fusion.6
  10.2 0.0 all-gather.7.cloned.1.call-update
  10.2 0.0 all-gather.9.cloned.1.call-start
  10.3 0.0 copy-done
  10.3 0.3 copy.16
  10.6 0.0 copy-done.5
  10.6 0.9 fusion.5
  11.4 0.0 all-gather.9.cloned.1.call-update
  11.5 0.0 all-gather.11.cloned.1.call-start
  11.5 0.0 copy-done.6
  11.5 0.0 copy-done.1
  11.5 0.9 fusion.4
  12.4 0.0 all-gather.11.cloned.1.call-update
  12.4 0.0 reduce-scatter.2.cloned.1.call-start
  12.5 0.0 copy-done.3
  12.5 0.1 copy.17
  12.6 0.0 copy-done.4
  12.6 0.1 copy.18
  12.8 0.0 copy-done.2
  12.8 1.1 gather_fusion.1
  14.0 1.1 gather_fusion.2
  15.1 0.2 select_reduce_fusion
  15.3 9.4 %all-gather.5.cloned.1.call-done = bf16[384,5120]{1,0:T(8,128)(2,1)} async-done(((bf16[384,2560]{1,0:T(8,128)(2,1)}), bf16[384,5120]{1,0:T(8,128)(2,1)}) %all-gather.5.cloned.1.call-update) | async-done | bytes 3932176 | tf_op jit(solution)/shard_map/all_gather | solution.py:17
  24.7 12.6 %gather_fusion = bf16[384,5120]{1,0:T(8,128)(2,1)} fusion(bf16[384,5120]{1,0:T(8,128)(2,1)} %all-gather.5.cloned.1.call-done, s32[1024]{0:T(1024)S(1)} %pad_clamp_fusion), kind=kCustom, calls=%fused_computation | custom fusion | bytes 7865856 | tf_op jit(solution)/shard_map/jit(_take)/gather | solution.py:20
  37.4 59.2 %all-gather.7.cloned.1.call-done = bf16[5120,384]{0,1:T(8,128)(2,1)} async-done(((bf16[640,384]{0,1:T(8,128)(2,1)}), bf16[5120,384]{0,1:T(8,128)(2,1)}) %all-gather.7.cloned.1.call-update) | async-done | bytes 3932176 | tf_op jit(solution)/shard_map/all_gather | solution.py:31
  96.5 5.5 %fusion.1 = f32[384,384]{1,0:T(8,128)S(1)} fusion(bf16[5120,384]{0,1:T(8,128)(2,1)} %all-gather.7.cloned.1.call-done, bf16[384,5120]{1,0:T(8,128)(2,1)} %gather_fusion, pred[384]{0:T(512)(128)(4,1)S(1)} %broadcast_compare_fusion), kind=kOutput, calls=%fused_computation.7 | convolution fusion | flops 1511915520 | bytes 8454528 | tf_op jit(solution)/shard_map/dot_general | solution.py:27
  102.1 65.2 %all-gather.9.cloned.1.call-done = bf16[5120,384]{0,1:T(8,128)(2,1)} async-done(((bf16[640,384]{0,1:T(8,128)(2,1)}), bf16[5120,384]{0,1:T(8,128)(2,1)}) %all-gather.9.cloned.1.call-update) | async-done | bytes 3932176 | tf_op jit(solution)/shard_map/all_gather | solution.py:32
  167.3 70.6 %all-gather.11.cloned.1.call-done = bf16[384,5120]{1,0:T(8,128)(2,1)} async-done(((bf16[384,640]{1,0:T(8,128)(2,1)}), bf16[384,5120]{1,0:T(8,128)(2,1)}) %all-gather.11.cloned.1.call-update) | async-done | bytes 3932176 | tf_op jit(solution)/shard_map/all_gather | solution.py:34
  237.9 10.7 %multiply_convert_fusion = bf16[384,5120]{1,0:T(8,128)(2,1)} fusion(bf16[384,5120]{1,0:T(8,128)(2,1)} %all-gather.11.cloned.1.call-done, f32[384]{0:T(512)S(1)} %compare_select_fusion.1, bf16[5120,384]{0,1:T(8,128)(2,1)} %all-gather.9.cloned.1.call-done, bf16[384,5120]{1,0:T(8,128)(2,1)} %gather_fusion, pred[384]{0:T(512)(128)(4,1)S(1)} %broadcast_compare_fusion, ...), kind=kOutput, calls=%fused_computation.4 | convolution fusion | flops 3026681856 | bytes 16320384 | tf_op jit(solution)/shard_map/dot_general | solution.py:36
  248.7 0.0 reduce-scatter.2.cloned.1.call-update
  248.7 12.3 %reduce-scatter.2.cloned.1.call-done = bf16[384,2560]{1,0:T(8,128)(2,1)} async-done(((bf16[384,5120]{1,0:T(8,128)(2,1)}), bf16[384,2560]{1,0:T(8,128)(2,1)}) %reduce-scatter.2.cloned.1.call-update) | async-done | bytes 1966096 | tf_op jit(solution)/shard_map/reduce_scatter | solution.py:38
  260.9 5.9 %scatter_custom_fusion = bf16[384,2560]{1,0:T(8,128)(2,1)} fusion(s32[384]{0:T(512)S(1)} %get-tuple-element.6, bf16[384,2560]{1,0:T(8,128)(2,1)} %reduce-scatter.2.cloned.1.call-done, bf16[]{:T(256)} %constant.33.clone.1), kind=kCustom, calls=%fused_computation.16 | custom fusion | bytes 1966592 | tf_op jit(solution)/shard_map/scatter | solution.py:45
  (4 shorter events, 0.0 us)
Async XLA Ops:
  6.5 3.8 %copy-start = (bf16[640,384]{1,0:T(8,128)(2,1)S(1)}, bf16[640,384]{1,0:T(8,128)(2,1)}, u32[]{:S(2)}) copy-start(bf16[640,384]{1,0:T(8,128)(2,1)} %param.16) | copy-start | bytes 1474564
  6.5 4.0 %copy-start.5 = (f32[640,3]{0,1:T(4,128)S(1)}, f32[640,3]{0,1:T(4,128)}, u32[]{:S(2)}) copy-start(f32[640,3]{0,1:T(4,128)} %param.17) | copy-start | bytes 23044
  6.5 5.0 %copy-start.6 = (f32[3,640]{1,0:T(4,128)S(1)}, f32[3,640]{1,0:T(4,128)}, u32[]{:S(2)}) copy-start(f32[3,640]{1,0:T(4,128)} %param.19) | copy-start | bytes 23044
  6.5 5.0 %copy-start.1 = (bf16[384,640]{1,0:T(8,128)(2,1)S(1)}, bf16[384,640]{1,0:T(8,128)(2,1)}, u32[]{:S(2)}) copy-start(bf16[384,640]{1,0:T(8,128)(2,1)} %param.18) | copy-start | bytes 1474564
  6.5 5.9 %copy-start.3 = (s32[384,6]{0,1:T(8,128)S(1)}, s32[384,6]{0,1:T(8,128)}, u32[]{:S(2)}) copy-start(s32[384,6]{0,1:T(8,128)} %param.11) | copy-start | bytes 27652
  6.5 6.1 %copy-start.4 = (f32[384,6]{0,1:T(8,128)S(1)}, f32[384,6]{0,1:T(8,128)}, u32[]{:S(2)}) copy-start(f32[384,6]{0,1:T(8,128)} %param.12) | copy-start | bytes 27652
  6.6 6.2 %copy-start.2 = (s32[384]{0:T(512)S(1)}, s32[384]{0:T(512)}, u32[]{:S(2)}) copy-start(s32[384]{0:T(512)} %param.13) | copy-start | bytes 4612
  6.6 18.2 %all-gather.5.cloned.1.call-start = ((), (), s32[]{:S(2)}) async-start(), calls=%async_computation.1 | async-start | bytes 5898240 | tf_op jit(solution)/shard_map/all_gather | solution.py:17
  7.3 89.2 %all-gather.7.cloned.1.call-start = ((), (), s32[]{:S(2)}) async-start(), calls=%async_computation.2 | async-start | bytes 4423680 | tf_op jit(solution)/shard_map/all_gather | solution.py:31
  10.2 157.1 %all-gather.9.cloned.1.call-start = ((), (), s32[]{:S(2)}) async-start(), calls=%async_computation.3 | async-start | bytes 4423680 | tf_op jit(solution)/shard_map/all_gather | solution.py:32
  11.5 226.5 %all-gather.11.cloned.1.call-start = ((), (), s32[]{:S(2)}) async-start(), calls=%async_computation.4 | async-start | bytes 4423680 | tf_op jit(solution)/shard_map/all_gather | solution.py:34
  12.4 248.5 %reduce-scatter.2.cloned.1.call-start = ((), (), s32[]{:S(2)}) async-start(), calls=%async_computation.5 | async-start | bytes 5898240 | tf_op jit(solution)/shard_map/reduce_scatter | solution.py:38
Sparse Core Ops, SparseCore 0:
  8.9 15.7 all-gather.4
  27.0 69.5 all-gather.6
  98.8 68.4 all-gather.8
  169.4 68.4 all-gather.10
  248.8 12.0 reduce-scatter.1
where the time goes:
time: 274 us; the launch traced here: 273 us
  waiting for transfers between devices  217 us (79%)
  local copies, waits for them, and re-layouts  22.7 us (8%)
  matrix products  16.2 us (6%)
  between operations  13.3 us (5%)
  other arithmetic  3.57 us (1%)
    all_gather x1, waiting for transfers between devices, body(): lax.all_gather(dequantize(down_q, down_scale, 0), 'dp', axis=1, tiled=True)  70.6 us
    all_gather x1, waiting for transfers between devices, body(): up_act = add_ready(lax.all_gather(up_local, 'dp', axis=0, tiled=True))  65.2 us
    all_gather x1, waiting for transfers between devices, body(): gate_act = add_ready(lax.all_gather(gate_local, 'dp', axis=0, tiled=True))  59.2 us
    gather x1, local copies, waits for them, and re-layouts, body(): routed_rows = jnp.take(full_tokens, safe_rows, axis=0)  12.6 us
    reduce_scatter x1, waiting for transfers between devices, body(): lax.psum_scatter(partial_value.astype(jnp.bfloat16), 'tensor', scatter_di...  12.3 us
    dot_general x1, matrix products, body(): jnp.dot(hidden, down_w, preferred_element_type=jnp.float32)  10.7 us
    all_gather x1, waiting for transfers between devices, body(): full_tokens = lax.all_gather(tokens, 'tensor', axis=1, tiled=True)  9.39 us
    scatter x1, local copies, waits for them, and re-layouts, body(): return jnp.zeros(shares.shape, jnp.bfloat16).at[target_row].set(shares.as...  5.94 us
  transfers between devices with their start and end apart: 5, of which 5 were waited for; matrix products, arithmetic and copies ran while one was open for 9% of the time, Pallas kernels for 0%

commit v1 on v0

v1 whole, which is shorter than its diff:
```python
import functools

import jax
import jax.numpy as jnp
from jax import lax
from jax.experimental import pallas as pl
from jax.experimental.pallas import tpu as pltpu
from jax.sharding import PartitionSpec as P

MESH = pl.DeviceIdType.MESH
F32 = jnp.float32
BF16 = jnp.bfloat16


def dequantize(values, scales, tile_axis):
    tile_len = values.shape[tile_axis] // scales.shape[tile_axis]
    return (values.astype(F32) * jnp.repeat(scales, tile_len, axis=tile_axis)).astype(BF16)


def general_body(
    tokens, expert_ids, combine, row_list, gate_q, gate_scale, up_q, up_scale, down_q, down_scale
):
    del row_list
    full_tokens = lax.all_gather(tokens, "tensor", axis=1, tiled=True)
    row_weight = jnp.sum(jnp.where(expert_ids == 0, combine, 0.0), axis=1)
    gate_w = lax.all_gather(dequantize(gate_q, gate_scale, 1), "dp", axis=0, tiled=True)
    up_w = lax.all_gather(dequantize(up_q, up_scale, 1), "dp", axis=0, tiled=True)
    down_w = lax.all_gather(dequantize(down_q, down_scale, 0), "dp", axis=1, tiled=True)
    gate_act = jnp.dot(full_tokens, gate_w, preferred_element_type=F32)
    up_act = jnp.dot(full_tokens, up_w, preferred_element_type=F32)
    hidden = (jax.nn.silu(gate_act) * up_act).astype(BF16)
    part = jnp.dot(hidden, down_w, preferred_element_type=F32) * row_weight[:, None]
    return lax.psum_scatter(part.astype(BF16), "tensor", scatter_dimension=1, tiled=True)


def kernel(
    nx, nz,
    tok, ids, comb, gq, gs, uq, us, dq, ds,
    out,
    T, W, D, acc, ps, pr, hid, o_own, o_send, o_recv,
    st_send, st_recv, sl, w_send, wx_send, w_recv, d_send, dx_send, dy_send, d_recv,
    p_send, p_recv, q_send, q_recv,
):
    y = lax.axis_index("groups")
    dp = lax.axis_index("dp")
    t = lax.axis_index("tensor")
    z, x = dp // nx, dp % nx
    oy, ot, ox = 1 - y, 1 - t, 1 - x
    rows = out.shape[0]
    half = W.shape[2]
    hd = D.shape[2]
    blk = D.shape[3]
    per_core = nx * nz // 2
    up_ok, down_ok = z < nz - 1, z > 0
    ydev, tdev, xdev = (oy, dp, t), (y, dp, ot), (y, z * nx + ox, t)
    zdev = ((y, dp + nx, t), (y, dp - nx, t))
    zok = (up_ok, down_ok)

    barrier = pltpu.get_barrier_semaphore()
    for dev in (ydev, tdev, xdev):
        pl.semaphore_signal(barrier, inc=1, device_id=dev, device_id_type=MESH)
    for k in range(2):
        @pl.when(zok[k])
        def _():
            pl.semaphore_signal(barrier, inc=1, device_id=zdev[k], device_id_type=MESH)

    def remote(src, dst, s, r, dev):
        return pltpu.make_async_remote_copy(
            src_ref=src, dst_ref=dst, send_sem=s, recv_sem=r, device_id=dev, device_id_type=MESH
        )

    own_tok = pltpu.make_async_copy(tok.at[y], T.at[0, 0], sl)
    tok_y = remote(tok.at[oy], T.at[0, 1], st_send.at[0], st_recv.at[0], ydev)
    tok_t = remote(tok.at[y], T.at[1, 0], st_send.at[1], st_recv.at[1], tdev)
    tok_f = remote(T.at[0, 1], T.at[1, 1], st_send.at[2], st_recv.at[2], tdev)
    own_tok.start()

    def wz(m, k, s):
        b = (z - s if k == 0 else z + s) * nx + x
        return remote(W.at[m, b], W.at[m, b], w_send.at[m, k, s], w_recv.at[m, b], zdev[k])

    def wx(m, zz):
        b = zz * nx + x
        return remote(W.at[m, b], W.at[m, b], wx_send.at[m, zz], w_recv.at[m, b], xdev)

    def w_wait(m, b):
        remote(W.at[m, b], W.at[m, b], wx_send.at[m, 0], w_recv.at[m, b], xdev).wait_recv()

    def dz(h, k, s):
        b = (z - s if k == 0 else z + s) * nx + x
        return remote(D.at[b, h], D.at[b, h], d_send.at[h, k, s], d_recv.at[b, h], zdev[k])

    def dx(zz):
        b = zz * nx + x
        return remote(D.at[b, y], D.at[b, y], dx_send.at[zz], d_recv.at[b, y], xdev)

    def dy(zz):
        b = zz * nx + ox
        return remote(D.at[b, y], D.at[b, y], dy_send.at[zz], d_recv.at[b, y], ydev)

    def d_wait(b, h):
        remote(D.at[b, h], D.at[b, h], dx_send.at[0], d_recv.at[b, h], xdev).wait_recv()

    def scale_block(m, q, s):
        for j in range(s.shape[1]):
            cols = pl.ds(j * 128, 128)
            v = q[pl.ds(y * half, half), cols].astype(F32)
            W[m, dp, :, cols] = (v * s[pl.ds(y * half, half), j : j + 1]).astype(BF16)

    scale_block(0, gq, gs)
    pl.semaphore_wait(barrier, 3 + jnp.where(up_ok, 1, 0) + jnp.where(down_ok, 1, 0))

    def start_own_w(m):
        for k in range(2):
            @pl.when(zok[k])
            def _():
                wz(m, k, 0).start()
        wx(m, z).start()

    start_own_w(0)
    tok_y.start()
    tok_t.start()
    scale_block(1, uq, us)
    start_own_w(1)
    for j in range(ds.shape[0]):
        lo = j * 128
        v = (dq[lo : lo + 128, :].astype(F32) * ds[j : j + 1, :]).astype(BF16)
        while lo < (j + 1) * 128:
            n = min((j + 1) * 128, (lo // hd + 1) * hd) - lo
            D[dp, lo // hd, lo % hd : lo % hd + n, :] = v[lo - j * 128 : lo - j * 128 + n]
            lo += n

    def each_arrival(s, body):
        if s >= nz:
            return

        @pl.when(z - s >= 0)
        def _():
            body(z - s, 0)

        @pl.when(z + s < nz)
        def _():
            body(z + s, 1)

    def w_event(m, s):
        def body(zz, k):
            w_wait(m, zz * nx + x)

            @pl.when(zok[k])
            def _():
                wz(m, k, s).start()

            wx(m, zz).start()

        each_arrival(s, body)

    def start_own_d():
        for i in range(2):
            h = y if i == 0 else oy
            for k in range(2):
                @pl.when(zok[k])
                def _():
                    dz(h, k, 0).start()
            if i == 0:
                dx(z).start()

    def d_event(s):
        def body(zz, k):
            b = zz * nx + x
            for i in range(2):
                h = y if i == 0 else oy
                d_wait(b, h)

                @pl.when(zok[k])
                def _():
                    dz(h, k, s).start()

                if i == 0:
                    dx(zz).start()

        each_arrival(s, body)

    def dy_event(s):
        def body(zz, k):
            d_wait(zz * nx + ox, y)
            dy(zz).start()

        if s == 0:
            body(z, 0)
        else:
            each_arrival(s, body)

    tile = 192

    def partial_act(m):
        for zz in range(nz):
            w_wait(m, zz * nx + ox)
        for who in (1, 0):
            @pl.loop(0, rows // tile)
            def _(i):
                r = pl.ds(pl.multiple_of(i * tile, tile), tile)
                total = None
                for side in range(2):
                    blocks = pl.ds((t if side == 0 else ot) * per_core, per_core)
                    w = W[m, blocks].reshape(per_core * half, W.shape[3])
                    p = jnp.dot(T[side, who, r, :], w, preferred_element_type=F32)
                    total = p if total is None else total + p
                if who == 1:
                    ps[m, r, :] = total.astype(BF16)
                else:
                    acc[m, r, :] = total
            if who == 1:
                pcopy(m).start()

    def pcopy(m):
        return remote(ps.at[m], pr.at[m], p_send.at[m], p_recv.at[m], ydev)

    w_event(0, 1)
    w_event(0, 2)
    w_event(0, 3)
    start_own_d()
    w_event(1, 1)
    tok_y.wait_recv()
    tok_f.start()
    own_tok.wait()
    tok_t.wait_recv()
    w_event(1, 2)
    w_event(1, 3)
    tok_f.wait_recv()
    partial_act(0)
    d_event(1)
    partial_act(1)
    dy_event(0)
    d_event(2)
    dy_event(1)
    for m in range(2):
        pcopy(m).wait_recv()
    for i in range(rows // tile):
        r = slice(i * tile, (i + 1) * tile)
        g = acc[0, r, :] + pr[0, r, :].astype(F32)
        u = acc[1, r, :] + pr[1, r, :].astype(F32)
        hid[r, :] = (g / (1.0 + jnp.exp(-g)) * u).astype(BF16)
    weight = jnp.sum(jnp.where(ids[...] == 0, comb[...], 0.0), axis=1, keepdims=True)

    def qcopy(c):
        return remote(o_send.at[c], o_recv.at[c], q_send.at[c], q_recv.at[c], tdev)

    def down_block(b):
        c = b % per_core
        mine = b // per_core == t
        w = D[b].reshape(2 * hd, blk)
        p = jnp.dot(hid[...], w, preferred_element_type=F32) * weight
        p = p.astype(BF16)

        @pl.when(mine)
        def _():
            o_own[c] = p

        @pl.when(jnp.logical_not(mine))
        def _():
            o_send[c] = p
            qcopy(c).start()

    d_event(3)
    dy_event(2)
    dy_event(3)

    @pl.loop(0, nz)
    def _(k):
        down_block(((z + k) % nz) * nx + x)

    @pl.loop(0, nz)
    def _(k):
        zz = (z + k) % nz
        d_wait(zz * nx + ox, oy)
        down_block(zz * nx + ox)

    for c in range(per_core):
        qcopy(c).wait_recv()
        cols = pl.ds(c * blk, blk)
        out[:, cols] = (o_own[c].astype(F32) + o_recv[c].astype(F32)).astype(BF16)

    tok_y.wait_send()
    tok_t.wait_send()
    tok_f.wait_send()
    for k in range(2):
        for s in range(nz - 1):
            here = (z - s >= 0) if k == 0 else (z + s < nz)

            @pl.when(jnp.logical_and(here, zok[k]))
            def _():
                for m in range(2):
                    wz(m, k, s).wait_send()
                for h in range(2):
                    dz(h, k, s).wait_send()
    for zz in range(nz):
        for m in range(2):
            wx(m, zz).wait_send()
        dx(zz).wait_send()
        dy(zz).wait_send()
    for m in range(2):
        pcopy(m).wait_send()
    for c in range(per_core):
        qcopy(c).wait_send()


def pair_body(
    tokens, expert_ids, combine, row_list, gate_q, gate_scale, up_q, up_scale, down_q, down_scale,
    *, nx, nz
):
    del row_list
    rows, feats = tokens.shape
    depth, width = gate_q.shape
    half = depth // 2
    blocks = nx * nz
    per_core = blocks // 2
    hd = down_q.shape[0] // 2
    blk = down_q.shape[1]
    tok = tokens.reshape(rows, per_core, 2, half).transpose(2, 0, 1, 3).reshape(2, rows, feats // 2)
    vmem = pl.BlockSpec(memory_space=pltpu.VMEM)
    dma = pltpu.SemaphoreType.DMA
    return pl.pallas_call(
        functools.partial(kernel, nx, nz),
        out_shape=jax.ShapeDtypeStruct((rows, feats), BF16),
        in_specs=[pl.BlockSpec(memory_space=pl.ANY)] + [vmem] * 8,
        out_specs=vmem,
        scratch_shapes=[
            pltpu.VMEM((2, 2, rows, feats // 2), BF16),
            pltpu.VMEM((2, blocks, half, width), BF16),
            pltpu.VMEM((blocks, 2, hd, blk), BF16),
            pltpu.VMEM((2, rows, width), F32),
            pltpu.VMEM((2, rows, width), BF16),
            pltpu.VMEM((2, rows, width), BF16),
            pltpu.VMEM((rows, width), BF16),
            pltpu.VMEM((per_core, rows, blk), BF16),
            pltpu.VMEM((per_core, rows, blk), BF16),
            pltpu.VMEM((per_core, rows, blk), BF16),
            dma((3,)), dma((3,)), dma,
            dma((2, 2, nz)), dma((2, nz)), dma((2, blocks)),
            dma((2, 2, nz)), dma((nz,)), dma((nz,)), dma((blocks, 2)),
            dma((2,)), dma((2,)), dma((per_core,)), dma((per_core,)),
        ],
        compiler_params=pltpu.CompilerParams(
            collective_id=0, has_side_effects=True, vmem_limit_bytes=56 * 1024 * 1024
        ),
        cost_estimate=pl.CostEstimate(
            flops=6 * rows * width * depth * blocks, bytes_accessed=40_000_000, transcendentals=rows * width
        ),
    )(tok, expert_ids, combine, gate_q, gate_scale, up_q, up_scale, down_q, down_scale)


def solution(mesh):
    placed = (
        P(("groups", "dp"), "tensor"),
        P(("groups", "dp"), None),
        P(("groups", "dp"), None),
        P(("groups", "dp")),
        P("dp", "tensor"),
        P("dp", "tensor"),
        P("dp", "tensor"),
        P("dp", "tensor"),
        P("tensor", "dp"),
        P("tensor", "dp"),
    )
    sizes = tuple(mesh.shape[a] for a in ("groups", "dp", "tensor"))
    body = functools.partial(pair_body, nx=2, nz=4) if sizes == (2, 8, 2) else general_body
    return jax.shard_map(
        body, mesh=mesh, in_specs=placed, out_specs=P(("groups", "dp"), "tensor"), check_vma=False
    )
```

time: 274 us -> 109 us (0.40)
  waiting for transfers between devices: 217 us -> 0 us
  Pallas kernels: 0 us -> 91.2 us
  matrix products: 16.2 us -> 0 us
  between operations: 13.3 us -> 0.02 us
  local copies, waits for them, and re-layouts: 22.7 us -> 17.3 us
  other arithmetic: 3.57 us -> 0 us
    all_gather x4 -> x0, waiting for transfers between devices: 204 us -> none  [the longest x1 70.6 us: body(): lax.all_gather(dequantize(down_q, down_scale, 0), 'dp', axis=1, tiled=True)]
    pallas_call x0 -> x1, Pallas kernels: none -> 91.2 us  [pair_body(): pl.pallas_call(functools.partial(kernel, nx, nz), out_shape=jax.ShapeDtyp...]
    dot_general x2 -> x0, matrix products: 16.2 us -> none  [the longest x1 10.7 us: body(): jnp.dot(hidden, down_w, preferred_element_type=jnp.float32)]
    gather x3 -> x0, local copies, waits for them, and re-layouts: 14.9 us -> none  [the longest x1 12.6 us: body(): routed_rows = jnp.take(full_tokens, safe_rows, axis=0)]
    reduce_scatter x1 -> x0, waiting for transfers between devices: 12.3 us -> none  [body(): lax.psum_scatter(partial_value.astype(jnp.bfloat16), 'tensor', scatter_di...]
    unnamed x18 -> x6, local copies, waits for them, and re-layouts: 1.84 us -> 13.1 us
    scatter x1 -> x0, local copies, waits for them, and re-layouts: 5.94 us -> none  [body(): return jnp.zeros(shares.shape, jnp.bfloat16).at[target_row].set(shares.as...]
    convert_element_type x3 -> x0, other arithmetic: 3.32 us -> none  [dequantize(): (values.astype(jnp.float32) * jnp.repeat(scales, tile_len, axis=tile_axis...]
  transfers between devices with their start and end apart: 5 -> 0, of which waited for: 5 -> 0; matrix products, arithmetic and copies ran while one was open for 9% -> 0% of each run, Pallas kernels for 0% -> 0%
where the time goes in v1:
time: 109 us
  Pallas kernels  91.2 us (84%)
  local copies, waits for them, and re-layouts  17.3 us (16%)
    pallas_call x1, Pallas kernels, pair_body(): pl.pallas_call(functools.partial(kernel, nx, nz), out_shape=jax.ShapeDtyp...  91.2 us
    unnamed x6, local copies, waits for them, and re-layouts  13.1 us
    reshape x1, local copies, waits for them, and re-layouts, pair_body(): tokens.reshape(rows, per_core, 2, half).transpose(2, 0, 1, 3)  2.4 us

profile of v1, /device:TPU:1, one launch (start us, length us, event | category | flops | bytes accessed | tf_op | source)
XLA Modules:
  0.0 108.5 jit_solution(16043050339761810191)
XLA Ops:
  0.0 1.5 %copy.18.ids = s32[384,6]{1,0:T(8,128)} copy(s32[384,6]{0,1:T(8,128)} %param.11) | data formatting | bytes 18432 | tf_op args[1]
  1.5 1.5 %copy.19.comb = f32[384,6]{1,0:T(8,128)} copy(f32[384,6]{0,1:T(8,128)} %param.12) | data formatting | bytes 18432 | tf_op args[2]
  3.0 1.6 %copy.20.gs = f32[640,3]{1,0:T(8,128)} copy(f32[640,3]{0,1:T(4,128)} %param.14) | data formatting | bytes 15360 | tf_op args[5]
  4.7 1.6 %copy.21.us = f32[640,3]{1,0:T(8,128)} copy(f32[640,3]{0,1:T(4,128)} %param.16) | data formatting | bytes 15360 | tf_op args[7]
  6.3 3.9 %copy.15 = bf16[384,2560]{0,1:T(8,128)(2,1)} copy(bf16[384,2560]{1,0:T(8,128)(2,1)} %param.10) | data formatting | bytes 3932160 | tf_op args[0]
  10.2 1.7 %copy.16 = bf16[2,384,4,320]{1,3,2,0:T(8,128)(2,1)S(1)} copy(bf16[2,384,4,320]{1,3,0,2:T(8,128)(2,1)} %bitcast.5) | data formatting | bytes 3932160 | tf_op jit(solution)/shard_map/transpose | solution.py:319
  11.9 2.4 %copy.17.tok = bf16[2,384,1280]{2,1,0:T(8,128)(2,1)} copy(bf16[2,384,1280]{1,2,0:T(8,128)(2,1)S(1)} %bitcast.4) | data formatting | bytes 3932160 | tf_op jit(solution)/shard_map/reshape | solution.py:319
  14.3 91.2 %shard_map.91 = bf16[384,2560]{1,0:T(8,128)(2,1)} custom-call(bf16[2,384,1280]{2,1,0:T(8,128)(2,1)} %copy.17.tok, s32[384,6]{1,0:T(8,128)} %copy.18.ids, f32[384,6]{1,0:T(8,128)} %copy.19.comb, bf16[640,384]{1,0:T(8,128)(2,1)} %gq.1, f32[640,3]{1,0:T(8,128)} %copy.20.gs, bf16[640,384]{1,0:T(8,128)(2,1)} %uq.1, f32[640,3]{1,0:T(8,128)} %copy.21.us, ...), custom_call_target="tpu_custom_call" | custom-call | flops 4529848320 | bytes 40000000 | tf_op jit(solution)/shard_map/pallas_call | solution.py:322
  105.6 2.9 %copy.23 = bf16[384,2560]{1,0:T(8,128)(2,1)} copy(bf16[384,2560]{1,0:T(8,128)(2,1)} %shard_map.91) | data formatting | bytes 3932160

commit v2 on v1

--- a/solution.py
+++ b/solution.py
@@ -37,8 +37,8 @@
     nx, nz,
     tok, ids, comb, gq, gs, uq, us, dq, ds,
     out,
-    T, W, D, acc, ps, pr, hid, o_own, o_send, o_recv,
-    st_send, st_recv, sl, w_send, wx_send, w_recv, d_send, dx_send, dy_send, d_recv,
+    T, W, D, wt, acc, ps, pr, hid, o_own, o_send, o_recv,
+    st_send, st_recv, f_send, f_recv, sl, w_send, wx_send, w_recv, d_send, dx_send, dy_send, d_recv,
     p_send, p_recv, q_send, q_recv,
 ):
     y = lax.axis_index("groups")
@@ -47,7 +47,12 @@
     z, x = dp // nx, dp % nx
     oy, ot, ox = 1 - y, 1 - t, 1 - x
     rows = out.shape[0]
-    half = W.shape[2]
+    win = W.shape[2]
+    depth = gq.shape[0]
+    half = depth // 2
+    pad = win - half
+    real = pl.ds(pl.multiple_of(y * pad, pad), half)
+    zero = pl.ds(pl.multiple_of((1 - y) * half, pad), pad)
     hd = D.shape[2]
     blk = D.shape[3]
     per_core = nx * nz // 2
@@ -69,22 +74,38 @@
             src_ref=src, dst_ref=dst, send_sem=s, recv_sem=r, device_id=dev, device_id_type=MESH
         )
 
-    own_tok = pltpu.make_async_copy(tok.at[y], T.at[0, 0], sl)
-    tok_y = remote(tok.at[oy], T.at[0, 1], st_send.at[0], st_recv.at[0], ydev)
-    tok_t = remote(tok.at[y], T.at[1, 0], st_send.at[1], st_recv.at[1], tdev)
-    tok_f = remote(T.at[0, 1], T.at[1, 1], st_send.at[2], st_recv.at[2], tdev)
-    own_tok.start()
+    def feats(j, v):
+        return tok.at[:, pl.ds(pl.multiple_of(j * depth + v * (depth - win), 128), win)]
+
+    def slot(side, who, j):
+        return T.at[side, who, :, pl.ds(j * win, win)]
+
+    def own_tok(j):
+        return pltpu.make_async_copy(feats(j, y), slot(0, 0, j), sl.at[j])
+
+    def tok_y(j):
+        return remote(feats(j, oy), slot(0, 1, j), st_send.at[0, j], st_recv.at[0, j], ydev)
+
+    def tok_t(j):
+        return remote(feats(j, y), slot(1, 0, j), st_send.at[1, j], st_recv.at[1, j], tdev)
+
+    tok_f = remote(T.at[0, 1], T.at[1, 1], f_send, f_recv, tdev)
+    for j in range(per_core):
+        own_tok(j).start()
 
     def wz(m, k, s):
         b = (z - s if k == 0 else z + s) * nx + x
-        return remote(W.at[m, b], W.at[m, b], w_send.at[m, k, s], w_recv.at[m, b], zdev[k])
+        ref = W.at[m, b, real]
+        return remote(ref, ref, w_send.at[m, k, s], w_recv.at[m, b], zdev[k])
 
     def wx(m, zz):
         b = zz * nx + x
-        return remote(W.at[m, b], W.at[m, b], wx_send.at[m, zz], w_recv.at[m, b], xdev)
+        ref = W.at[m, b, real]
+        return remote(ref, ref, wx_send.at[m, zz], w_recv.at[m, b], xdev)
 
     def w_wait(m, b):
-        remote(W.at[m, b], W.at[m, b], wx_send.at[m, 0], w_recv.at[m, b], xdev).wait_recv()
+        ref = W.at[m, b, real]
+        remote(ref, ref, wx_send.at[m, 0], w_recv.at[m, b], xdev).wait_recv()
 
     def dz(h, k, s):
         b = (z - s if k == 0 else z + s) * nx + x
@@ -101,11 +122,15 @@
     def d_wait(b, h):
         remote(D.at[b, h], D.at[b, h], dx_send.at[0], d_recv.at[b, h], xdev).wait_recv()
 
+    def spread(row):
+        return jnp.broadcast_to(row, (128, row.shape[1])).T
+
     def scale_block(m, q, s):
-        for j in range(s.shape[1]):
+        first = pl.multiple_of(y * (depth - win), 128)
+        for j in range(s.shape[0]):
             cols = pl.ds(j * 128, 128)
-            v = q[pl.ds(y * half, half), cols].astype(F32)
-            W[m, dp, :, cols] = (v * s[pl.ds(y * half, half), j : j + 1]).astype(BF16)
+            v = q[pl.ds(first, win), cols].astype(F32)
+            W[m, dp, :, cols] = (v * spread(s[j : j + 1, pl.ds(first, win)])).astype(BF16)
 
     scale_block(0, gq, gs)
     pl.semaphore_wait(barrier, 3 + jnp.where(up_ok, 1, 0) + jnp.where(down_ok, 1, 0))
@@ -118,8 +143,9 @@
         wx(m, z).start()
 
     start_own_w(0)
-    tok_y.start()
-    tok_t.start()
+    for j in range(per_core):
+        tok_y(j).start()
+        tok_t(j).start()
     scale_block(1, uq, us)
     start_own_w(1)
     for j in range(ds.shape[0]):
@@ -202,7 +228,7 @@
                 total = None
                 for side in range(2):
                     blocks = pl.ds((t if side == 0 else ot) * per_core, per_core)
-                    w = W[m, blocks].reshape(per_core * half, W.shape[3])
+                    w = W[m, blocks].reshape(per_core * win, W.shape[3])
                     p = jnp.dot(T[side, who, r, :], w, preferred_element_type=F32)
                     total = p if total is None else total + p
                 if who == 1:
@@ -215,15 +241,23 @@
     def pcopy(m):
         return remote(ps.at[m], pr.at[m], p_send.at[m], p_recv.at[m], ydev)
 
+    for m in range(2):
+        @pl.loop(0, nx * nz)
+        def _(b):
+            W[m, b, zero] = jnp.zeros((pad, W.shape[3]), BF16)
+    wt[...] = spread(jnp.sum(jnp.where(ids[...] == 0, comb[...], 0.0), axis=0, keepdims=True))
+
     w_event(0, 1)
     w_event(0, 2)
     w_event(0, 3)
     start_own_d()
     w_event(1, 1)
-    tok_y.wait_recv()
+    for j in range(per_core):
+        tok_y(j).wait_recv()
     tok_f.start()
-    own_tok.wait()
-    tok_t.wait_recv()
+    for j in range(per_core):
+        own_tok(j).wait()
+        tok_t(j).wait_recv()
     w_event(1, 2)
     w_event(1, 3)
     tok_f.wait_recv()
@@ -240,7 +274,6 @@
         g = acc[0, r, :] + pr[0, r, :].astype(F32)
         u = acc[1, r, :] + pr[1, r, :].astype(F32)
         hid[r, :] = (g / (1.0 + jnp.exp(-g)) * u).astype(BF16)
-    weight = jnp.sum(jnp.where(ids[...] == 0, comb[...], 0.0), axis=1, keepdims=True)
 
     def qcopy(c):
         return remote(o_send.at[c], o_recv.at[c], q_send.at[c], q_recv.at[c], tdev)
@@ -249,16 +282,18 @@
         c = b % per_core
         mine = b // per_core == t
         w = D[b].reshape(2 * hd, blk)
-        p = jnp.dot(hid[...], w, preferred_element_type=F32) * weight
-        p = p.astype(BF16)
+        p = jnp.dot(hid[...], w, preferred_element_type=F32)
+        p = [(p[:, i : i + 128] * wt[...]).astype(BF16) for i in range(0, blk, 128)]
 
         @pl.when(mine)
         def _():
-            o_own[c] = p
+            for i, v in enumerate(p):
+                o_own[c, :, i * 128 : (i + 1) * 128] = v
 
         @pl.when(jnp.logical_not(mine))
         def _():
-            o_send[c] = p
+            for i, v in enumerate(p):
+                o_send[c, :, i * 128 : (i + 1) * 128] = v
             qcopy(c).start()
 
     d_event(3)
@@ -280,8 +315,9 @@
         cols = pl.ds(c * blk, blk)
         out[:, cols] = (o_own[c].astype(F32) + o_recv[c].astype(F32)).astype(BF16)
 
-    tok_y.wait_send()
-    tok_t.wait_send()
+    for j in range(per_core):
+        tok_y(j).wait_send()
+        tok_t(j).wait_send()
     tok_f.wait_send()
     for k in range(2):
         for s in range(nz - 1):
@@ -311,12 +347,11 @@
     del row_list
     rows, feats = tokens.shape
     depth, width = gate_q.shape
-    half = depth // 2
+    win = -(-(depth // 2) // 128) * 128
     blocks = nx * nz
     per_core = blocks // 2
     hd = down_q.shape[0] // 2
     blk = down_q.shape[1]
-    tok = tokens.reshape(rows, per_core, 2, half).transpose(2, 0, 1, 3).reshape(2, rows, feats // 2)
     vmem = pl.BlockSpec(memory_space=pltpu.VMEM)
     dma = pltpu.SemaphoreType.DMA
     return pl.pallas_call(
@@ -325,9 +360,10 @@
         in_specs=[pl.BlockSpec(memory_space=pl.ANY)] + [vmem] * 8,
         out_specs=vmem,
         scratch_shapes=[
-            pltpu.VMEM((2, 2, rows, feats // 2), BF16),
-            pltpu.VMEM((2, blocks, half, width), BF16),
+            pltpu.VMEM((2, 2, rows, per_core * win), BF16),
+            pltpu.VMEM((2, blocks, win, width), BF16),
             pltpu.VMEM((blocks, 2, hd, blk), BF16),
+            pltpu.VMEM((rows, 128), F32),
             pltpu.VMEM((2, rows, width), F32),
             pltpu.VMEM((2, rows, width), BF16),
             pltpu.VMEM((2, rows, width), BF16),
@@ -335,18 +371,18 @@
             pltpu.VMEM((per_core, rows, blk), BF16),
             pltpu.VMEM((per_core, rows, blk), BF16),
             pltpu.VMEM((per_core, rows, blk), BF16),
-            dma((3,)), dma((3,)), dma,
+            dma((2, per_core)), dma((2, per_core)), dma, dma, dma((per_core,)),
             dma((2, 2, nz)), dma((2, nz)), dma((2, blocks)),
             dma((2, 2, nz)), dma((nz,)), dma((nz,)), dma((blocks, 2)),
             dma((2,)), dma((2,)), dma((per_core,)), dma((per_core,)),
         ],
         compiler_params=pltpu.CompilerParams(
-            collective_id=0, has_side_effects=True, vmem_limit_bytes=56 * 1024 * 1024
+            collective_id=0, has_side_effects=True, vmem_limit_bytes=40 * 1024 * 1024
         ),
         cost_estimate=pl.CostEstimate(
             flops=6 * rows * width * depth * blocks, bytes_accessed=40_000_000, transcendentals=rows * width
         ),
-    )(tok, expert_ids, combine, gate_q, gate_scale, up_q, up_scale, down_q, down_scale)
+    )(tokens, expert_ids.T, combine.T, gate_q, gate_scale.T, up_q, up_scale.T, down_q, down_scale)
 
 
 def solution(mesh):

time: 109 us -> 98.6 us (0.905)
  local copies, waits for them, and re-layouts: 17.3 us -> 9.42 us
  Pallas kernels: 91.2 us -> 88.6 us
    unnamed x6 -> x19, local copies, waits for them, and re-layouts: 13.1 us -> 9.42 us
    pallas_call x1, Pallas kernels: 91.2 us -> 88.6 us  [pair_body(): pl.pallas_call(functools.partial(kernel, nx, nz), out_shape=jax.ShapeDtyp...]
    reshape x1 -> x0, local copies, waits for them, and re-layouts: 2.4 us -> none  [pair_body(): tokens.reshape(rows, per_core, 2, half).transpose(2, 0, 1, 3)]
    transpose x1 -> x0, local copies, waits for them, and re-layouts: 1.74 us -> none  [pair_body(): tokens.reshape(rows, per_core, 2, half).transpose(2, 0, 1, 3)]
where the time goes in v2:
time: 98.6 us; the launch traced here: 98 us
  Pallas kernels  88.6 us (90%)
  local copies, waits for them, and re-layouts  9.42 us (10%)
    pallas_call x1, Pallas kernels, pair_body(): pl.pallas_call(functools.partial(kernel, nx, nz), out_shape=jax.ShapeDtyp...  88.6 us
    unnamed x19, local copies, waits for them, and re-layouts  9.42 us

profile of v2, /device:TPU:1, one launch (start us, length us, event | category | flops | bytes accessed | tf_op | source)
XLA Modules:
  0.0 98.0 jit_solution(10416362525377215738)
XLA Ops:
  0.0 0.0 copy-start
  0.0 1.5 %copy-done = bf16[384,2560]{1,0:T(8,128)(2,1)S(1)} copy-done((bf16[384,2560]{1,0:T(8,128)(2,1)S(1)}, bf16[384,2560]{1,0:T(8,128)(2,1)}, u32[]{:S(2)}) %copy-start) | copy-done | bytes 1966104
  1.5 0.0 copy-start.1
  1.5 1.0 %copy-done.1 = bf16[640,384]{1,0:T(8,128)(2,1)S(1)} copy-done((bf16[640,384]{1,0:T(8,128)(2,1)S(1)}, bf16[640,384]{1,0:T(8,128)(2,1)}, u32[]{:S(2)}) %copy-start.1) | copy-done | bytes 491544
  2.6 0.0 copy-start.2
  2.6 1.0 %copy-done.2 = bf16[640,384]{1,0:T(8,128)(2,1)S(1)} copy-done((bf16[640,384]{1,0:T(8,128)(2,1)S(1)}, bf16[640,384]{1,0:T(8,128)(2,1)}, u32[]{:S(2)}) %copy-start.2) | copy-done | bytes 491544
  3.6 0.0 copy-start.3
  3.6 1.0 %copy-done.3 = bf16[384,640]{1,0:T(8,128)(2,1)S(1)} copy-done((bf16[384,640]{1,0:T(8,128)(2,1)S(1)}, bf16[384,640]{1,0:T(8,128)(2,1)}, u32[]{:S(2)}) %copy-start.3) | copy-done | bytes 491544
  4.6 0.0 copy-start.4
  4.6 0.7 copy-done.4
  5.3 0.0 copy-start.5
  5.3 0.7 copy-done.5
  6.1 0.0 copy-start.6
  6.1 0.7 copy-done.6
  6.8 0.0 copy-start.7
  6.8 0.7 copy-done.7
  7.5 0.0 copy-start.8
  7.5 0.7 copy-done.8
  8.2 88.6 %shard_map.91 = bf16[384,2560]{1,0:T(8,128)(2,1)S(1)} custom-call(bf16[384,2560]{1,0:T(8,128)(2,1)S(1)} %copy-done, s32[6,384]{1,0:T(8,128)S(1)} %bitcast.4, f32[6,384]{1,0:T(8,128)S(1)} %bitcast.5, bf16[640,384]{1,0:T(8,128)(2,1)S(1)} %copy-done.1, f32[3,640]{1,0:T(4,128)S(1)} %bitcast.6, bf16[640,384]{1,0:T(8,128)(2,1)S(1)} %copy-done.2, ...), custom_call_target="tpu_custom_call" | custom-call | flops 4529848320 | bytes 40000000 | tf_op jit(solution)/shard_map/pallas_call | solution.py:357
  96.8 1.3 %copy.11 = bf16[384,2560]{1,0:T(8,128)(2,1)} copy(bf16[384,2560]{1,0:T(8,128)(2,1)S(1)} %shard_map.91) | data formatting | bytes 3932160
Async XLA Ops:
  0.0 1.5 %copy-start = (bf16[384,2560]{1,0:T(8,128)(2,1)S(1)}, bf16[384,2560]{1,0:T(8,128)(2,1)}, u32[]{:S(2)}) copy-start(bf16[384,2560]{1,0:T(8,128)(2,1)} %tok.1) | copy-start | bytes 5898244
  1.5 1.0 %copy-start.1 = (bf16[640,384]{1,0:T(8,128)(2,1)S(1)}, bf16[640,384]{1,0:T(8,128)(2,1)}, u32[]{:S(2)}) copy-start(bf16[640,384]{1,0:T(8,128)(2,1)} %gq.1) | copy-start | bytes 1474564
  2.6 1.0 %copy-start.2 = (bf16[640,384]{1,0:T(8,128)(2,1)S(1)}, bf16[640,384]{1,0:T(8,128)(2,1)}, u32[]{:S(2)}) copy-start(bf16[640,384]{1,0:T(8,128)(2,1)} %uq.1) | copy-start | bytes 1474564
  3.6 1.0 %copy-start.3 = (bf16[384,640]{1,0:T(8,128)(2,1)S(1)}, bf16[384,640]{1,0:T(8,128)(2,1)}, u32[]{:S(2)}) copy-start(bf16[384,640]{1,0:T(8,128)(2,1)} %dq.1) | copy-start | bytes 1474564
  4.6 0.7 copy-start.4
  5.3 0.7 copy-start.5
  6.1 0.7 copy-start.6
  6.8 0.7 copy-start.7
  7.5 0.7 copy-start.8

commit v3 on v2

--- a/solution.py
+++ b/solution.py
@@ -35,9 +35,9 @@
 
 def kernel(
     nx, nz,
-    tok, ids, comb, gq, gs, uq, us, dq, ds,
+    tok, ids_h, comb_h, gq_h, gs_h, uq_h, us_h, dq_h, ds_h,
     out,
-    T, W, D, wt, acc, ps, pr, hid, o_own, o_send, o_recv,
+    gs, gq, us, uq, ds, dq, ids, comb, in_sem, T, W, D, wt, acc, ps, pr, hid, o_own, o_send, o_recv,
     st_send, st_recv, f_send, f_recv, sl, w_send, wx_send, w_recv, d_send, dx_send, dy_send, d_recv,
     p_send, p_recv, q_send, q_recv,
 ):
@@ -61,6 +61,12 @@
     zdev = ((y, dp + nx, t), (y, dp - nx, t))
     zok = (up_ok, down_ok)
 
+    sources = (gs_h, gq_h, us_h, uq_h, ds_h, dq_h, ids_h, comb_h)
+    targets = (gs, gq, us, uq, ds, dq, ids, comb)
+    loads = [pltpu.make_async_copy(a, b, in_sem.at[i]) for i, (a, b) in enumerate(zip(sources, targets))]
+    for load in loads:
+        load.start()
+
     barrier = pltpu.get_barrier_semaphore()
     for dev in (ydev, tdev, xdev):
         pl.semaphore_signal(barrier, inc=1, device_id=dev, device_id_type=MESH)
@@ -132,6 +138,8 @@
             v = q[pl.ds(first, win), cols].astype(F32)
             W[m, dp, :, cols] = (v * spread(s[j : j + 1, pl.ds(first, win)])).astype(BF16)
 
+    loads[0].wait()
+    loads[1].wait()
     scale_block(0, gq, gs)
     pl.semaphore_wait(barrier, 3 + jnp.where(up_ok, 1, 0) + jnp.where(down_ok, 1, 0))
 
@@ -146,8 +154,12 @@
     for j in range(per_core):
         tok_y(j).start()
         tok_t(j).start()
+    loads[2].wait()
+    loads[3].wait()
     scale_block(1, uq, us)
     start_own_w(1)
+    loads[4].wait()
+    loads[5].wait()
     for j in range(ds.shape[0]):
         lo = j * 128
         v = (dq[lo : lo + 128, :].astype(F32) * ds[j : j + 1, :]).astype(BF16)
@@ -180,29 +192,22 @@
 
         each_arrival(s, body)
 
-    def start_own_d():
-        for i in range(2):
-            h = y if i == 0 else oy
-            for k in range(2):
-                @pl.when(zok[k])
-                def _():
-                    dz(h, k, 0).start()
-            if i == 0:
-                dx(z).start()
-
-    def d_event(s):
+    def start_own_d(h):
+        for k in range(2):
+            @pl.when(zok[k])
+            def _():
+                dz(h, k, 0).start()
+
+    def d_event(h, s, cross):
         def body(zz, k):
-            b = zz * nx + x
-            for i in range(2):
-                h = y if i == 0 else oy
-                d_wait(b, h)
-
-                @pl.when(zok[k])
-                def _():
-                    dz(h, k, s).start()
-
-                if i == 0:
-                    dx(zz).start()
+            d_wait(zz * nx + x, h)
+
+            @pl.when(zok[k])
+            def _():
+                dz(h, k, s).start()
+
+            if cross:
+                dx(zz).start()
 
         each_arrival(s, body)
 
@@ -245,12 +250,15 @@
         @pl.loop(0, nx * nz)
         def _(b):
             W[m, b, zero] = jnp.zeros((pad, W.shape[3]), BF16)
+    loads[6].wait()
+    loads[7].wait()
     wt[...] = spread(jnp.sum(jnp.where(ids[...] == 0, comb[...], 0.0), axis=0, keepdims=True))
 
     w_event(0, 1)
     w_event(0, 2)
+    start_own_d(y)
     w_event(0, 3)
-    start_own_d()
+    dx(z).start()
     w_event(1, 1)
     for j in range(per_core):
         tok_y(j).wait_recv()
@@ -258,15 +266,20 @@
     for j in range(per_core):
         own_tok(j).wait()
         tok_t(j).wait_recv()
+    d_event(y, 1, True)
     w_event(1, 2)
-    w_event(1, 3)
     tok_f.wait_recv()
     partial_act(0)
-    d_event(1)
+    dy_event(0)
+    w_event(1, 3)
+    d_event(y, 2, True)
+    start_own_d(oy)
+    dy_event(1)
+    d_event(y, 3, True)
+    d_event(oy, 1, False)
     partial_act(1)
-    dy_event(0)
-    d_event(2)
-    dy_event(1)
+    dy_event(2)
+    d_event(oy, 2, False)
     for m in range(2):
         pcopy(m).wait_recv()
     for i in range(rows // tile):
@@ -296,17 +309,21 @@
                 o_send[c, :, i * 128 : (i + 1) * 128] = v
             qcopy(c).start()
 
-    d_event(3)
-    dy_event(2)
+    def nearest(k):
+        low = jnp.where(k <= z, z - k, k)
+        high = jnp.where(k <= nz - 1 - z, z + k, nz - 1 - k)
+        return jnp.where(2 * z < nz, low, high)
+
     dy_event(3)
+    d_event(oy, 3, False)
 
     @pl.loop(0, nz)
     def _(k):
-        down_block(((z + k) % nz) * nx + x)
+        down_block(nearest(k) * nx + x)
 
     @pl.loop(0, nz)
     def _(k):
-        zz = (z + k) % nz
+        zz = nearest(k)
         d_wait(zz * nx + ox, oy)
         down_block(zz * nx + ox)
 
@@ -357,9 +374,18 @@
     return pl.pallas_call(
         functools.partial(kernel, nx, nz),
         out_shape=jax.ShapeDtypeStruct((rows, feats), BF16),
-        in_specs=[pl.BlockSpec(memory_space=pl.ANY)] + [vmem] * 8,
+        in_specs=[pl.BlockSpec(memory_space=pltpu.HBM)] * 9,
         out_specs=vmem,
         scratch_shapes=[
+            pltpu.VMEM(gate_scale.shape[::-1], F32),
+            pltpu.VMEM(gate_q.shape, BF16),
+            pltpu.VMEM(up_scale.shape[::-1], F32),
+            pltpu.VMEM(up_q.shape, BF16),
+            pltpu.VMEM(down_scale.shape, F32),
+            pltpu.VMEM(down_q.shape, BF16),
+            pltpu.VMEM(expert_ids.shape[::-1], jnp.int32),
+            pltpu.VMEM(combine.shape[::-1], F32),
+            dma((8,)),
             pltpu.VMEM((2, 2, rows, per_core * win), BF16),
             pltpu.VMEM((2, blocks, win, width), BF16),
             pltpu.VMEM((blocks, 2, hd, blk), BF16),
@@ -377,7 +403,7 @@
             dma((2,)), dma((2,)), dma((per_core,)), dma((per_core,)),
         ],
         compiler_params=pltpu.CompilerParams(
-            collective_id=0, has_side_effects=True, vmem_limit_bytes=40 * 1024 * 1024
+            collective_id=0, has_side_effects=True, vmem_limit_bytes=56 * 1024 * 1024
         ),
         cost_estimate=pl.CostEstimate(
             flops=6 * rows * width * depth * blocks, bytes_accessed=40_000_000, transcendentals=rows * width

time: 98.6 us -> 87.2 us (0.88)
  local copies, waits for them, and re-layouts: 9.42 us -> 2.94 us
  Pallas kernels: 88.6 us -> 84.1 us
    unnamed x19 -> x1, local copies, waits for them, and re-layouts: 9.42 us -> 2.94 us
    pallas_call x1, Pallas kernels: 88.6 us -> 84.1 us  [pair_body(): pl.pallas_call(functools.partial(kernel, nx, nz), out_shape=jax.ShapeDtyp...]
where the time goes in v3:
time: 87.2 us; the launch traced here: 87 us
  Pallas kernels  84.1 us (96%)
  local copies, waits for them, and re-layouts  2.94 us (3%)
    pallas_call x1, Pallas kernels, pair_body(): pl.pallas_call(functools.partial(kernel, nx, nz), out_shape=jax.ShapeDtyp...  84.1 us
    unnamed x1, local copies, waits for them, and re-layouts  2.94 us

profile of v3, /device:TPU:1, one launch (start us, length us, event | category | flops | bytes accessed | tf_op | source)
XLA Modules:
  0.0 87.0 jit_solution(8146498788481688454)
XLA Ops:
  0.0 84.1 %shard_map.91 = bf16[384,2560]{1,0:T(8,128)(2,1)} custom-call(bf16[384,2560]{1,0:T(8,128)(2,1)} %tok.1, s32[6,384]{1,0:T(8,128)} %bitcast.4, f32[6,384]{1,0:T(8,128)} %bitcast.5, bf16[640,384]{1,0:T(8,128)(2,1)} %gq_h.1, f32[3,640]{1,0:T(4,128)} %bitcast.6, bf16[640,384]{1,0:T(8,128)(2,1)} %uq_h.1, f32[3,640]{1,0:T(4,128)} %bitcast.7, ...), custom_call_target="tpu_custom_call" | custom-call | flops 4529848320 | bytes 40000000 | tf_op jit(solution)/shard_map/pallas_call | solution.py:374
  84.1 2.9 %copy.11 = bf16[384,2560]{1,0:T(8,128)(2,1)} copy(bf16[384,2560]{1,0:T(8,128)(2,1)} %shard_map.91) | data formatting | bytes 3932160

commit v4 on v3

--- a/solution.py
+++ b/solution.py
@@ -48,7 +48,7 @@
     oy, ot, ox = 1 - y, 1 - t, 1 - x
     rows = out.shape[0]
     win = W.shape[2]
-    depth = gq.shape[0]
+    depth, width = gq.shape
     half = depth // 2
     pad = win - half
     real = pl.ds(pl.multiple_of(y * pad, pad), half)
@@ -99,34 +99,41 @@
     for j in range(per_core):
         own_tok(j).start()
 
+    cut = width - width % 256 if width % 256 else width // 2
+    pieces = ((0, 0, width), (1, 0, cut), (1, cut, width - cut))
+
+    def wref(m, b):
+        i, lo, n = pieces[m]
+        return W.at[i, b, real, pl.ds(lo, n)]
+
     def wz(m, k, s):
         b = (z - s if k == 0 else z + s) * nx + x
-        ref = W.at[m, b, real]
+        ref = wref(m, b)
         return remote(ref, ref, w_send.at[m, k, s], w_recv.at[m, b], zdev[k])
 
     def wx(m, zz):
         b = zz * nx + x
-        ref = W.at[m, b, real]
+        ref = wref(m, b)
         return remote(ref, ref, wx_send.at[m, zz], w_recv.at[m, b], xdev)
 
     def w_wait(m, b):
-        ref = W.at[m, b, real]
+        ref = wref(m, b)
         remote(ref, ref, wx_send.at[m, 0], w_recv.at[m, b], xdev).wait_recv()
 
-    def dz(h, k, s):
+    def dz(q, k, s):
         b = (z - s if k == 0 else z + s) * nx + x
-        return remote(D.at[b, h], D.at[b, h], d_send.at[h, k, s], d_recv.at[b, h], zdev[k])
-
-    def dx(zz):
-        b = zz * nx + x
-        return remote(D.at[b, y], D.at[b, y], dx_send.at[zz], d_recv.at[b, y], xdev)
-
-    def dy(zz):
-        b = zz * nx + ox
-        return remote(D.at[b, y], D.at[b, y], dy_send.at[zz], d_recv.at[b, y], ydev)
-
-    def d_wait(b, h):
-        remote(D.at[b, h], D.at[b, h], dx_send.at[0], d_recv.at[b, h], xdev).wait_recv()
+        return remote(D.at[b, q], D.at[b, q], d_send.at[q, k, s], d_recv.at[b, q], zdev[k])
+
+    def dx(zz, i):
+        b, q = zz * nx + x, 2 * y + i
+        return remote(D.at[b, q], D.at[b, q], dx_send.at[zz, i], d_recv.at[b, q], xdev)
+
+    def dy(zz, i):
+        b, q = zz * nx + ox, 2 * y + i
+        return remote(D.at[b, q], D.at[b, q], dy_send.at[zz, i], d_recv.at[b, q], ydev)
+
+    def d_wait(b, q):
+        remote(D.at[b, q], D.at[b, q], dx_send.at[0, 0], d_recv.at[b, q], xdev).wait_recv()
 
     def spread(row):
         return jnp.broadcast_to(row, (128, row.shape[1])).T
@@ -143,12 +150,13 @@
     scale_block(0, gq, gs)
     pl.semaphore_wait(barrier, 3 + jnp.where(up_ok, 1, 0) + jnp.where(down_ok, 1, 0))
 
-    def start_own_w(m):
+    def start_own_w(m, along_x=True):
         for k in range(2):
             @pl.when(zok[k])
             def _():
                 wz(m, k, 0).start()
-        wx(m, z).start()
+        if along_x:
+            wx(m, z).start()
 
     start_own_w(0)
     for j in range(per_core):
@@ -193,28 +201,31 @@
         each_arrival(s, body)
 
     def start_own_d(h):
-        for k in range(2):
-            @pl.when(zok[k])
-            def _():
-                dz(h, k, 0).start()
+        for i in range(2):
+            for k in range(2):
+                @pl.when(zok[k])
+                def _():
+                    dz(2 * h + i, k, 0).start()
 
     def d_event(h, s, cross):
         def body(zz, k):
-            d_wait(zz * nx + x, h)
-
-            @pl.when(zok[k])
-            def _():
-                dz(h, k, s).start()
-
-            if cross:
-                dx(zz).start()
+            for i in range(2):
+                d_wait(zz * nx + x, 2 * h + i)
+
+                @pl.when(zok[k])
+                def _():
+                    dz(2 * h + i, k, s).start()
+
+                if cross:
+                    dx(zz, i).start()
 
         each_arrival(s, body)
 
     def dy_event(s):
         def body(zz, k):
-            d_wait(zz * nx + ox, y)
-            dy(zz).start()
+            for i in range(2):
+                d_wait(zz * nx + ox, 2 * y + i)
+                dy(zz, i).start()
 
         if s == 0:
             body(z, 0)
@@ -224,6 +235,8 @@
     tile = 192
 
     def partial_act(m):
+        mat, lo, n = pieces[m]
+        cols = pl.ds(lo, n)
         for zz in range(nz):
             w_wait(m, zz * nx + ox)
         for who in (1, 0):
@@ -233,18 +246,20 @@
                 total = None
                 for side in range(2):
                     blocks = pl.ds((t if side == 0 else ot) * per_core, per_core)
-                    w = W[m, blocks].reshape(per_core * win, W.shape[3])
+                    w = W[mat, blocks, :, cols].reshape(per_core * win, n)
                     p = jnp.dot(T[side, who, r, :], w, preferred_element_type=F32)
                     total = p if total is None else total + p
                 if who == 1:
-                    ps[m, r, :] = total.astype(BF16)
+                    ps[mat, r, cols] = total.astype(BF16)
                 else:
-                    acc[m, r, :] = total
+                    acc[mat, r, cols] = total
             if who == 1:
                 pcopy(m).start()
 
     def pcopy(m):
-        return remote(ps.at[m], pr.at[m], p_send.at[m], p_recv.at[m], ydev)
+        mat, lo, n = pieces[m]
+        cols = pl.ds(lo, n)
+        return remote(ps.at[mat, :, cols], pr.at[mat, :, cols], p_send.at[m], p_recv.at[m], ydev)
 
     for m in range(2):
         @pl.loop(0, nx * nz)
@@ -257,8 +272,10 @@
     w_event(0, 1)
     w_event(0, 2)
     start_own_d(y)
+    start_own_w(2, along_x=False)
     w_event(0, 3)
-    dx(z).start()
+    for i in range(2):
+        dx(z, i).start()
     w_event(1, 1)
     for j in range(per_core):
         tok_y(j).wait_recv()
@@ -272,15 +289,19 @@
     partial_act(0)
     dy_event(0)
     w_event(1, 3)
+    wx(2, z).start()
+    for s in range(1, nz):
+        w_event(2, s)
     d_event(y, 2, True)
+    dy_event(1)
     start_own_d(oy)
-    dy_event(1)
+    partial_act(1)
     d_event(y, 3, True)
     d_event(oy, 1, False)
-    partial_act(1)
+    partial_act(2)
     dy_event(2)
     d_event(oy, 2, False)
-    for m in range(2):
+    for m in range(len(pieces)):
         pcopy(m).wait_recv()
     for i in range(rows // tile):
         r = slice(i * tile, (i + 1) * tile)
@@ -294,7 +315,7 @@
     def down_block(b):
         c = b % per_core
         mine = b // per_core == t
-        w = D[b].reshape(2 * hd, blk)
+        w = D[b].reshape(D.shape[1] * hd, blk)
         p = jnp.dot(hid[...], w, preferred_element_type=F32)
         p = [(p[:, i : i + 128] * wt[...]).astype(BF16) for i in range(0, blk, 128)]
 
@@ -317,20 +338,27 @@
     dy_event(3)
     d_event(oy, 3, False)
 
+    def add_blocks(col):
+        for i in range(per_core // nx):
+            c = i * nx + col
+            qcopy(c).wait_recv()
+            total = o_own[c].astype(F32) + o_recv[c].astype(F32)
+            out[:, pl.ds(pl.multiple_of(c * blk, 128), blk)] = total.astype(BF16)
+
     @pl.loop(0, nz)
     def _(k):
         down_block(nearest(k) * nx + x)
 
+    add_blocks(x)
+
     @pl.loop(0, nz)
     def _(k):
         zz = nearest(k)
-        d_wait(zz * nx + ox, oy)
+        for i in range(2):
+            d_wait(zz * nx + ox, 2 * oy + i)
         down_block(zz * nx + ox)
 
-    for c in range(per_core):
-        qcopy(c).wait_recv()
-        cols = pl.ds(c * blk, blk)
-        out[:, cols] = (o_own[c].astype(F32) + o_recv[c].astype(F32)).astype(BF16)
+    add_blocks(ox)
 
     for j in range(per_core):
         tok_y(j).wait_send()
@@ -342,16 +370,17 @@
 
             @pl.when(jnp.logical_and(here, zok[k]))
             def _():
-                for m in range(2):
+                for m in range(len(pieces)):
                     wz(m, k, s).wait_send()
-                for h in range(2):
-                    dz(h, k, s).wait_send()
+                for q in range(4):
+                    dz(q, k, s).wait_send()
     for zz in range(nz):
-        for m in range(2):
+        for m in range(len(pieces)):
             wx(m, zz).wait_send()
-        dx(zz).wait_send()
-        dy(zz).wait_send()
-    for m in range(2):
+        for i in range(2):
+            dx(zz, i).wait_send()
+            dy(zz, i).wait_send()
+    for m in range(len(pieces)):
         pcopy(m).wait_send()
     for c in range(per_core):
         qcopy(c).wait_send()
@@ -367,7 +396,7 @@
     win = -(-(depth // 2) // 128) * 128
     blocks = nx * nz
     per_core = blocks // 2
-    hd = down_q.shape[0] // 2
+    hd = down_q.shape[0] // 4
     blk = down_q.shape[1]
     vmem = pl.BlockSpec(memory_space=pltpu.VMEM)
     dma = pltpu.SemaphoreType.DMA
@@ -388,7 +417,7 @@
             dma((8,)),
             pltpu.VMEM((2, 2, rows, per_core * win), BF16),
             pltpu.VMEM((2, blocks, win, width), BF16),
-            pltpu.VMEM((blocks, 2, hd, blk), BF16),
+            pltpu.VMEM((blocks, 4, hd, blk), BF16),
             pltpu.VMEM((rows, 128), F32),
             pltpu.VMEM((2, rows, width), F32),
             pltpu.VMEM((2, rows, width), BF16),
@@ -398,9 +427,9 @@
             pltpu.VMEM((per_core, rows, blk), BF16),
             pltpu.VMEM((per_core, rows, blk), BF16),
             dma((2, per_core)), dma((2, per_core)), dma, dma, dma((per_core,)),
-            dma((2, 2, nz)), dma((2, nz)), dma((2, blocks)),
-            dma((2, 2, nz)), dma((nz,)), dma((nz,)), dma((blocks, 2)),
-            dma((2,)), dma((2,)), dma((per_core,)), dma((per_core,)),
+            dma((3, 2, nz)), dma((3, nz)), dma((3, blocks)),
+            dma((4, 2, nz)), dma((nz, 2)), dma((nz, 2)), dma((blocks, 4)),
+            dma((3,)), dma((3,)), dma((per_core,)), dma((per_core,)),
         ],
         compiler_params=pltpu.CompilerParams(
             collective_id=0, has_side_effects=True, vmem_limit_bytes=56 * 1024 * 1024

time: 87.2 us -> 87.9 us (level)
  no operation moved by 1% of the time
where the time goes in v4:
time: 87.9 us; the launch traced here: 87.2 us
  Pallas kernels  84.2 us (96%)
  local copies, waits for them, and re-layouts  2.94 us (3%)
    pallas_call x1, Pallas kernels, pair_body(): pl.pallas_call(functools.partial(kernel, nx, nz), out_shape=jax.ShapeDtyp...  84.2 us
    unnamed x1, local copies, waits for them, and re-layouts  2.94 us

profile of v4, /device:TPU:1, one launch (start us, length us, event | category | flops | bytes accessed | tf_op | source)
XLA Modules:
  0.0 87.2 jit_solution(11733040223264881409)
XLA Ops:
  0.0 84.2 %shard_map.91 = bf16[384,2560]{1,0:T(8,128)(2,1)} custom-call(bf16[384,2560]{1,0:T(8,128)(2,1)} %tok.1, s32[6,384]{1,0:T(8,128)} %bitcast.4, f32[6,384]{1,0:T(8,128)} %bitcast.5, bf16[640,384]{1,0:T(8,128)(2,1)} %gq_h.1, f32[3,640]{1,0:T(4,128)} %bitcast.6, bf16[640,384]{1,0:T(8,128)(2,1)} %uq_h.1, f32[3,640]{1,0:T(4,128)} %bitcast.7, ...), custom_call_target="tpu_custom_call" | custom-call | flops 4529848320 | bytes 40000000 | tf_op jit(solution)/shard_map/pallas_call | solution.py:403
  84.2 2.9 %copy.11 = bf16[384,2560]{1,0:T(8,128)(2,1)} copy(bf16[384,2560]{1,0:T(8,128)(2,1)} %shard_map.91) | data formatting | bytes 3932160

commit v5 on v3

--- a/solution.py
+++ b/solution.py
@@ -157,7 +157,6 @@
     loads[2].wait()
     loads[3].wait()
     scale_block(1, uq, us)
-    start_own_w(1)
     loads[4].wait()
     loads[5].wait()
     for j in range(ds.shape[0]):
@@ -255,6 +254,7 @@
     wt[...] = spread(jnp.sum(jnp.where(ids[...] == 0, comb[...], 0.0), axis=0, keepdims=True))
 
     w_event(0, 1)
+    start_own_w(1)
     w_event(0, 2)
     start_own_d(y)
     w_event(0, 3)
@@ -317,9 +317,18 @@
     dy_event(3)
     d_event(oy, 3, False)
 
+    def add_blocks(col):
+        for i in range(per_core // nx):
+            c = i * nx + col
+            qcopy(c).wait_recv()
+            total = o_own[c].astype(F32) + o_recv[c].astype(F32)
+            out[:, pl.ds(pl.multiple_of(c * blk, 128), blk)] = total.astype(BF16)
+
     @pl.loop(0, nz)
     def _(k):
         down_block(nearest(k) * nx + x)
+
+    add_blocks(x)
 
     @pl.loop(0, nz)
     def _(k):
@@ -327,10 +336,7 @@
         d_wait(zz * nx + ox, oy)
         down_block(zz * nx + ox)
 
-    for c in range(per_core):
-        qcopy(c).wait_recv()
-        cols = pl.ds(c * blk, blk)
-        out[:, cols] = (o_own[c].astype(F32) + o_recv[c].astype(F32)).astype(BF16)
+    add_blocks(ox)
 
     for j in range(per_core):
         tok_y(j).wait_send()

time: 87.2 us -> 87.2 us (level)
  no operation moved by 1% of the time
where the time goes in v5:
time: 87.2 us; the launch traced here: 87 us
  Pallas kernels  84.1 us (96%)
  local copies, waits for them, and re-layouts  2.94 us (3%)
    pallas_call x1, Pallas kernels, pair_body(): pl.pallas_call(functools.partial(kernel, nx, nz), out_shape=jax.ShapeDtyp...  84.1 us
    unnamed x1, local copies, waits for them, and re-layouts  2.94 us

profile of v5, /device:TPU:1, one launch (start us, length us, event | category | flops | bytes accessed | tf_op | source)
XLA Modules:
  0.0 87.0 jit_solution(18138616892768147305)
XLA Ops:
  0.0 84.1 %shard_map.91 = bf16[384,2560]{1,0:T(8,128)(2,1)} custom-call(bf16[384,2560]{1,0:T(8,128)(2,1)} %tok.1, s32[6,384]{1,0:T(8,128)} %bitcast.4, f32[6,384]{1,0:T(8,128)} %bitcast.5, bf16[640,384]{1,0:T(8,128)(2,1)} %gq_h.1, f32[3,640]{1,0:T(4,128)} %bitcast.6, bf16[640,384]{1,0:T(8,128)(2,1)} %uq_h.1, f32[3,640]{1,0:T(4,128)} %bitcast.7, ...), custom_call_target="tpu_custom_call" | custom-call | flops 4529848320 | bytes 40000000 | tf_op jit(solution)/shard_map/pallas_call | solution.py:380
  84.1 2.9 %copy.11 = bf16[384,2560]{1,0:T(8,128)(2,1)} copy(bf16[384,2560]{1,0:T(8,128)(2,1)} %shard_map.91) | data formatting | bytes 3932160
